TPU v7x, 128 devices: a whole 4x4x4 slice. The times are simulated.
128 devices in a mesh: dp: 32 (over z, y, x_lo), tensor: 4 (over x_hi, core).
Axes of the slice: x: 4 (x_hi: 2, x_lo: 2; x = x_hi * 2 + x_lo), y: 4, z: 4, core: 2. Of those that a mesh axis runs over, the one named last changes fastest.
Arguments:
- tokens: bfloat16 [32, 1024, 1024], P('dp', 'tensor'), may hold values from -6 to 6
- doc_starts: int32 [32, 4], P('dp'), may hold values from 0 to 1023, as said below
- cotangent: bfloat16 [32, 1024, 1024], P('dp', 'tensor'), may hold values from -12 to 12
- w_query: bfloat16 [1024, 2048], P(None, 'tensor'), may hold values from -0.1875 to 0.1875
- key_matrix: bfloat16 [1024, 1024], P(None, 'tensor'), may hold values from -0.1875 to 0.1875
- value_matrix: bfloat16 [1024, 1024], P(None, 'tensor'), may hold values from -0.1875 to 0.1875
- w_out: bfloat16 [2048, 1024], P('tensor'), may hold values from -0.75 to 0.75
- w_gate: bfloat16 [1024, 3072], P(None, 'tensor'), may hold values from -0.1875 to 0.1875
- w_up: bfloat16 [1024, 3072], P(None, 'tensor'), may hold values from -0.1875 to 0.1875
- w_down: bfloat16 [3072, 1024], P('tensor'), may hold values from -0.21875 to 0.21875
- gain_attn: float32 [1024], replicated, may hold values from 0.5 to 1.5
- gain_mlp: float32 [1024], replicated, may hold values from 0.5 to 1.5
- gain_query: float32 [128], replicated, may hold values from 0.5 to 1.5
- gain_key: float32 [128], replicated, may hold values from 0.5 to 1.5
Outputs:
- layer_out: bfloat16 [32, 1024, 1024], P('dp', 'tensor')
- grad_tokens: float32 [32, 1024, 1024], P('dp', 'tensor')
- grad_w_query: float32 [1024, 2048], P('dp', 'tensor')
- grad_w_key: float32 [1024, 1024], P('dp', 'tensor')
- grad_w_value: float32 [1024, 1024], P('dp', 'tensor')
- grad_w_out: float32 [2048, 1024], P('tensor', 'dp')
- grad_w_gate: float32 [1024, 3072], P('dp', 'tensor')
- grad_w_up: float32 [1024, 3072], P('dp', 'tensor')
- grad_w_down: float32 [3072, 1024], P('tensor', 'dp')
- grad_gain_attn: float32 [1024], replicated
- grad_gain_mlp: float32 [1024], replicated
- grad_gain_query: float32 [128], replicated
- grad_gain_key: float32 [128], replicated
Inputs may be any that keep to these rules, and one draw needn't show every extreme that they name: `doc_starts`: each row lists the first tokens of 4 documents that tile a sequence of 1024 tokens in order: the first is 0 and they rise strictly. In each sequence one document, at a place drawn from the seed, starts before token 193 and reaches token 831; each other document has at most 64 tokens.
All inputs are finite; a program needn't handle non-finite values.
Results may differ from a plain program's by a relative error of at most 0.03.
Values may be sent and summed in bfloat16 or wider, within the bound.
A program may use at most 128 MiB of HBM per device.

v0:
```python
import math

import jax
import jax.numpy as jnp
import numpy as np
from jax import lax
from jax.experimental import pallas as pl
from jax.experimental.pallas import tpu as pltpu
from jax.sharding import PartitionSpec as P

MESH = pl.DeviceIdType.MESH
BF16 = jnp.bfloat16
F32 = jnp.float32
EPSILON = 1e-06
ROPE_BASE = 1000000.0
BLOCK = 256
HALF = 128
HEAD = 128
QUERY_SCALE = math.log2(math.e) / math.sqrt(HEAD)
PARTNERS = ("core", "far", "y1", "y2", "z1", "z2", "x")
DIAGONALS = (("y", 2), ("z", 2), ("tensor", "far_core"))
ORDERS = (("y1", "y2", "z1", "z2"), ("y2", "y1", "z2", "z1"), ("z1", "z2", "y1", "y2"), ("z2", "z1", "y2", "y1"))
MLP_STREAMS = (
    ("mlp_mix", 0, 640, 0, 0, 0, 1536),
    ("mlp_mix", 640, 640, 4, 0, 1, 2176),
    ("mlp_mix", 1280, 256, 8, 0, 2, 2816),
    ("t_gu", 0, 256, 8, 256, 2, 3072),
    ("t_gu", 256, 512, 12, 0, 3, 3328),
)
ATTN_STREAMS = tuple(("attn_mix", 384 * k, 384, 4 * k, 0, k, 384 * k) for k in range(4))
GAIN_ORDER = ("y", "z", "tensor", "x")

SCRATCH = (
    ("w_qkv", (1024, 1024), BF16),
    ("t_qkv", (1024, 1024), BF16),
    ("w_down", (768, 1024), BF16),
    ("t_gu", (6, 4, 64, 1024), BF16),
    ("mlp_mix", (4, 4, 64, 2304), BF16),
    ("attn_mix", (4, 4, 64, 1536), BF16),
    ("h1", (1024, 1024), BF16),
    ("h2", (1024, 1024), BF16),
    ("da", (1024, 1024), BF16),
    ("norm_qk", (768, 1024), BF16),
    ("root_qk", (8, 1024), F32),
    ("ob", (512, 1024), BF16),
    ("qs", (2, 4, 128, 512), BF16),
    ("ks_t", (256, 1024), BF16),
    ("ks", (2, 1024, 128), BF16),
    ("v_t", (2, 144, 1024), BF16),
    ("v", (2, 1024, 128), BF16),
    ("p", (20, 4, 64, 512), BF16),
    ("inv", (2, 4, 8, 512), F32),
    ("inner", (2, 4, 8, 512), F32),
    ("hidden", (768, 1024), BF16),
    ("dgu", (1536, 1024), BF16),
    ("cosine", (64, 1024), F32),
    ("sine", (64, 1024), F32),
    ("x_t", (1024, 256), BF16),
    ("resid", (1024, 256), F32),
    ("gain1", (1024, 128), F32),
    ("gain2", (1024, 128), F32),
    ("gain_q", (128, 128), F32),
    ("gain_k", (128, 128), F32),
    ("gain_sum", (1024, 128), F32),
    ("gain_q_sum", (128, 128), F32),
    ("gain_k_sum", (128, 256), F32),
    ("root1", (8, 256), F32),
    ("root2", (8, 256), F32),
    ("keep", (2, 1024, 256), F32),
    ("sib_out", (2, 2, 1024, 128), BF16),
    ("sib_in", (2, 2, 1024, 128), BF16),
    ("far_out", (2, 1024, 128), BF16),
    ("far_in", (2, 1024, 128), BF16),
    ("mlp_own", (1024, 256), F32),
    ("mlp_sib_out", (2, 2, 1024, 128), BF16),
    ("mlp_sib_in", (2, 2, 1024, 128), BF16),
    ("mlp_far_out", (2, 1024, 128), BF16),
    ("mlp_far_in", (2, 1024, 128), BF16),
    ("mlp_halves", (16, 4, 64, 640), BF16),
    ("sums", (32, 3840), F32),
    ("stage", (256, 1024), BF16),
    ("x_in", (256, 1024), BF16),
    ("g1_in", (1, 1024), F32),
    ("g2_in", (1, 1024), F32),
    ("gq_in", (1, 128), F32),
    ("gk_in", (1, 128), F32),
    ("frequency", (64, 128), F32),
    ("gain_own", (24, 128), F32),
    ("gain_parts", (4, 4, 24, 128), F32),
)
SEMAPHORES = 160


class Box:
    pass


class Place:
    def __init__(self):
        dp = lax.axis_index("dp")
        tensor = lax.axis_index("tensor")
        self.z, self.y, self.x = dp // 8, (dp // 2) % 4, dp % 2
        self.far, self.core = tensor // 2, tensor % 2
        self.me = tensor
        self.sib = self.far * 2 + 1 - self.core
        self.across = (1 - self.far) * 2 + self.core
        self.across_sib = (1 - self.far) * 2 + 1 - self.core

    def near(self, name):
        return step_of(name, self.y if name[0] == "y" else self.z)

    def along(self, name):
        return {"y": self.y, "z": self.z, "x": self.x, "tensor": self.me}[name]

    def device(self, name):
        z, y, x, far, core = self.z, self.y, self.x, self.far, self.core
        if isinstance(name, tuple):
            axis, steps = name
            if axis == "tensor":
                if steps == "far_core":
                    far, core = 1 - far, 1 - core
                else:
                    turned = (self.me + steps) % 4
                    far, core = turned // 2, turned % 2
            elif axis == "y":
                y = (y + steps) % 4
            elif axis == "z":
                z = (z + steps) % 4
            else:
                x = 1 - x
        elif name[0] == "y":
            y = self.near(name)
        elif name[0] == "z":
            z = self.near(name)
        elif name == "x":
            x = 1 - x
        elif name == "far":
            far = 1 - far
        else:
            core = 1 - core
        return ((z * 4 + y) * 2 + x, far * 2 + core)


def step_of(name, value):
    return value + 1 - 2 * (value % 2) if name[1] == "1" else 3 - value


def nn(left, right):
    return lax.dot_general(left, right, (((1,), (0,)), ((), ())), preferred_element_type=F32)


def nt(left, right):
    return lax.dot_general(left, right, (((1,), (1,)), ((), ())), preferred_element_type=F32)


def span(index, size=BLOCK):
    return pl.ds(pl.multiple_of(index * size, size), size)


def loop(count, body):
    def step(index, carry):
        body(index)
        return carry

    lax.fori_loop(0, count, step, 0)


def twice(values):
    return jnp.concatenate([values, values], axis=1)


def fold(values):
    return jnp.sum(values.reshape(values.shape[0] // 8, 8, values.shape[1]), axis=0)


def sub(block, part):
    return pl.ds(pl.multiple_of(block * BLOCK + part * HALF, HALF), HALF)


def lanes(part, size=128):
    return pl.ds(part * size if isinstance(part, int) else pl.multiple_of(part * size, size), size)


def steps(count, body):
    def step(index, carry):
        body(index, lambda k, act: pl.when(index == k)(act))
        return carry

    lax.fori_loop(0, count, step, 0)


class Copy:
    def __init__(self, links, src, dst, name, index):
        self.links, self.src, self.dst, self.name, self.index = links, src, dst, name, index

    def make(self):
        return pltpu.make_async_remote_copy(
            src_ref=self.src(),
            dst_ref=self.dst(),
            send_sem=self.links.sems.at[0, self.index],
            recv_sem=self.links.sems.at[1, self.index],
            device_id=self.links.place.device(self.name),
            device_id_type=MESH,
        )

    def start(self):
        self.make().start()

    def wait_recv(self):
        self.make().wait_recv()

    def wait_send(self):
        self.make().wait_send()


class Links:
    def __init__(self, place, sems):
        self.place, self.sems, self.used, self.sent = place, sems, 0, []

    def copy(self, src, dst, name):
        self.used += 1
        return Copy(self, src, dst, name, self.used - 1)

    def send(self, src, dst, name):
        copy = self.copy(src, dst, name)
        copy.start()
        return copy


class Gather:
    def __init__(self, links, at):
        place = links.place

        def copies(block, name):
            halves = [lambda part=part: at(block, part) for part in range(2)]
            return [links.copy(half, half, name) for half in halves]

        self.far, self.sib = copies(place.me, "far"), copies(place.me, "core")
        self.passed = copies(place.across, "core")

    def send_far(self, part):
        self.far[part].start()

    def send_near(self, part):
        self.sib[part].start()

    def send(self, part):
        self.send_far(part)
        self.send_near(part)

    def pass_on(self, part):
        self.far[part].wait_recv()
        self.passed[part].start()

    def near_ready(self, part):
        self.sib[part].wait_recv()

    def far_ready(self, part):
        self.passed[part].wait_recv()

    def drain(self):
        for copy in self.far + self.sib + self.passed:
            copy.wait_send()


class Reduce:
    def __init__(self, links, sib_out, sib_in, far_out, far_in):
        self.sib_in, self.far_out, self.far_in = sib_in, far_out, far_in
        self.copies = {}
        for part in range(2):
            for index in range(2):
                src = lambda at=(index, part): sib_out.at[at]
                dst = lambda at=(index, part): sib_in.at[at]
                self.copies[index, part] = links.copy(src, dst, "core")
            src, dst = lambda part=part: far_out.at[part], lambda part=part: far_in.at[part]
            self.copies[2, part] = links.copy(src, dst, "far")

    def to_sibling(self, index, part):
        self.copies[index, part].start()

    def make_far(self, keep, part):
        self.copies[0, part].wait_recv()

        def body(i):
            rows = span(i, 512)
            summed = keep[rows, lanes(part)] + self.sib_in[0, part, rows, :].astype(F32)
            self.far_out[part, rows, :] = summed.astype(BF16)

        loop(2, body)

    def send_far(self, part):
        self.copies[2, part].start()

    def arrive(self, part):
        self.copies[1, part].wait_recv()
        self.copies[2, part].wait_recv()

    def total(self, keep, part, rows):
        near = keep[rows, lanes(part)] + self.sib_in[1, part, rows, :].astype(F32)
        return near + self.far_in[part, rows, :].astype(F32)

    def release(self, index, part):
        self.copies.pop((index, part)).wait_send()

    def drain(self):
        for copy in self.copies.values():
            copy.wait_send()


class DpSum:
    def __init__(self, links, box, streams, bufs):
        self.links, self.bufs, self.out = links, bufs, box.sums
        self.streams = [(getattr(box, name), *rest) for name, *rest in streams]
        self.phase = -1
        self.flying = [[] for _ in streams]
        self.sent = []

    def spot(self, stream, slot, *rest):
        _, _, w, at, column, _, _ = self.streams[stream]
        lead = pl.ds(at + slot.start, slot.size) if isinstance(slot, pl.Slice) else at + slot
        return (lead, *rest, pl.ds(column, w))

    def held(self, stream, phase):
        every = slice(None)
        if phase == 0:
            spot = self.spot(stream, pl.ds(0, 2), every, every)
        elif phase == 1:
            spot = self.spot(stream, 2, every, every)
        elif phase == 2:
            spot = self.spot(stream, 3, pl.ds(0, 2), every)
        elif phase == 3:
            spot = self.spot(stream, 3, 2, every)
        else:
            spot = self.spot(stream, 3, 3, pl.ds(0, 32))
        return self.bufs.at[spot]

    def begin(self, stream, phase):
        place = self.links.place
        source_ref, first, w, _, _, order, _ = self.streams[stream]
        order = ORDERS[order]
        name = "x" if phase == 4 else order[phase]

        def other(j):
            there = place.near(name)
            return there if j == 0 else step_of(order[phase + 1], there)

        def source(j):
            if phase == 4:
                return self.bufs.at[self.spot(stream, 3, 2, span(1 - place.x, 32))]
            if phase in (1, 3):
                return self.held(stream, phase - 1).at[1]
            if phase == 2:
                return self.held(stream, 1).at[other(j)]
            lead = (pl.ds(0, 4), other(j)) if name[0] == "y" else (other(j), slice(None))
            return source_ref.at[(*lead, slice(None), pl.ds(first, w))]

        def into(j):
            whole = self.held(stream, phase)
            return whole.at[j] if phase in (0, 2) else whole

        count = 2 if phase in (0, 2) else 1
        send = self.links.send
        return [send(lambda j=j: source(j), lambda j=j: into(j), name) for j in range(count)]

    def finish(self, stream, phase):
        place, spot, bufs = self.links.place, self.spot, self.bufs
        source_ref, first, w, _, _, order, out_first = self.streams[stream]
        order = ORDERS[order]
        every = slice(None)
        for copy in self.flying[stream]:
            copy.wait_recv()
        if phase == 4:
            mine = bufs[spot(stream, 3, 2, span(place.x, 32))].astype(F32)
            columns = pl.ds(out_first, w)
            self.out[:, columns] = bufs[spot(stream, 3, 3, pl.ds(0, 32))].astype(F32) + mine
        elif phase == 3:
            bufs[spot(stream, 3, 2, every)] += bufs[spot(stream, 3, 0, every)]
        elif phase == 1:
            for k in range(4):
                bufs[spot(stream, 2, k, every)] += bufs[spot(stream, 0, k, every)]
        else:
            name = order[phase]
            mine = place.y if name[0] == "y" else place.z
            for j, own in enumerate((mine, step_of(order[phase + 1], mine))):
                if phase == 2:
                    bufs[spot(stream, 3, j, every)] += bufs[spot(stream, 2, own, every)]
                    continue
                for k in range(4):
                    lead = (k, own) if name[0] == "y" else (own, k)
                    kept = source_ref[(*lead, every, pl.ds(first, w))]
                    bufs[spot(stream, j, k, every)] += kept

    def start(self, *streams):
        for stream in streams:
            self.flying[stream] = self.begin(stream, 0)
        self.phase = 0

    def advance(self):
        if self.phase == 5:
            return
        for stream in range(len(self.streams)):
            self.finish(stream, self.phase)
            self.sent += self.flying[stream]
            if self.phase < 4:
                self.flying[stream] = self.begin(stream, self.phase + 1)
        self.phase += 1

    def complete(self):
        while self.phase < 5:
            self.advance()

    def drain(self):
        for copy in self.sent:
            copy.wait_send()


class GainSum:
    def __init__(self, links, own, parts):
        self.links, self.parts, self.copies, self.step = links, parts, [], 0
        self.begin(own[...])

    def begin(self, values):
        place, name = self.links.place, GAIN_ORDER[self.step]
        mine = place.along(name)
        half = self.parts.at[self.step, mine]
        self.parts[self.step, mine] = values
        count = 2 if name == "x" else 4
        self.copies.append([self.links.send(lambda: half, lambda: half, (name, k)) for k in range(1, count)])

    def advance(self):
        if self.step == 4:
            return
        for copy in self.copies[self.step]:
            copy.wait_recv()
        parts = [self.parts[self.step, k] for k in range(len(self.copies[self.step]) + 1)]
        total = parts[0] + parts[1]
        if len(parts) == 4:
            total = total + (parts[2] + parts[3])
        self.step += 1
        if self.step < 4:
            self.begin(total)
        else:
            self.total = total

    def drain(self):
        for copies in self.copies:
            for copy in copies:
                copy.wait_send()


def head_forward(raw, gain, cosine, sine):
    root = lax.rsqrt(jnp.mean(raw * raw, axis=0, keepdims=True) + EPSILON)
    normed = raw * root
    scaled = normed * gain
    first, second = scaled[:64], scaled[64:]
    turned = jnp.concatenate([first * cosine - second * sine, second * cosine + first * sine], axis=0)
    return normed, root, turned


def head_backward(grad, normed, root, gain, cosine, sine):
    first, second = grad[:64], grad[64:]
    turned = jnp.concatenate([first * cosine + second * sine, second * cosine - first * sine], axis=0)
    scaled = turned * gain
    inner = jnp.mean(scaled * normed, axis=0, keepdims=True)
    return root * (scaled - normed * inner), turned * normed


def layer_kernel(
    x, starts, dy, wq, wk, wv, wo, wg, wu, wd, g1, g2, gq, gk, frequency,
    out, grad_x, out_sums, out_gains,
    *scratch,
):
    s = Box()
    for (name, _, _), ref in zip(SCRATCH, scratch):
        setattr(s, name, ref)
    s.keep_far, s.keep_own = s.keep.at[0], s.keep.at[1]
    link_sems, load_sems, ready = scratch[len(SCRATCH) :]
    place = Place()
    links = Links(place, link_sems)
    me, sib, across, across_sib = place.me, place.sib, place.across, place.across_sib

    barrier = pltpu.get_barrier_semaphore()
    for name in PARTNERS + DIAGONALS:
        pl.semaphore_signal(barrier, inc=1, device_id=place.device(name), device_id_type=MESH)

    loads = []

    def load(src, dst):
        copy = pltpu.make_async_copy(src, dst, load_sems.at[len(loads)])
        copy.start()
        loads.append(copy)

    load(x, s.x_in)
    load(g1, s.g1_in)
    for g in range(2):
        load(wq.at[:, pl.ds(256 * g, 256)], s.w_qkv.at[:, pl.ds(512 * g, 256)])
        load(wk.at[:, pl.ds(128 * g, 128)], s.w_qkv.at[:, pl.ds(512 * g + 256, 128)])
        load(wv.at[:, pl.ds(128 * g, 128)], s.w_qkv.at[:, pl.ds(512 * g + 384, 128)])
    load(wo, s.h2.at[pl.ds(0, 512)])
    load(wg, s.mlp_mix.at[:, :, :, pl.ds(0, 768)])
    load(wu, s.mlp_mix.at[:, :, :, pl.ds(768, 768)])
    load(wd, s.w_down)
    load(dy, s.da.at[pl.ds(0, 256)])
    load(g2, s.g2_in)
    load(gq, s.gq_in)
    load(gk, s.gk_in)
    load(frequency, s.frequency)

    near_pair, far_pair = (sib, me), (across_sib, across)

    def pair(ref, rows, blocks, part):
        return jnp.concatenate([ref[rows, sub(b, part)] for b in blocks], axis=1)

    def unpair(ref, rows, blocks, part, values):
        for n, b in enumerate(blocks):
            ref[rows, sub(b, part)] = values[:, HALF * n : HALF * n + HALF]

    every = pl.ds(0, 1024)

    loads[0].wait()
    loads[1].wait()
    gather_h1 = Gather(links, lambda b, part: s.h1.at[:, sub(b, part)])
    for part in range(2):

        def first_norm(i, part=part):
            rows = span(2 * part + i, 64)
            xs = s.x_in[rows, :].astype(F32)
            root = lax.rsqrt(jnp.mean(xs * xs, axis=1, keepdims=True) + EPSILON)
            s.stage[rows, :] = (xs * root * s.g1_in[...]).astype(BF16)

        loop(2, first_norm)
        for j in range(4):
            s.h1[pl.ds(256 * j, 256), sub(me, part)] = s.stage[lanes(part), pl.ds(256 * j, 256)].T
        if part == 0:
            pl.semaphore_wait(barrier, len(PARTNERS) + len(DIAGONALS))
        gather_h1.send(part)

    for k in range(2, 8):
        loads[k].wait()

    def turn_qkv(i):
        s.t_qkv[span(i), :] = s.w_qkv[:, span(i)].T

    loop(4, turn_qkv)

    for k in range(13, 17):
        loads[k].wait()
    place_row = lax.broadcasted_iota(jnp.int32, (8, 1024), 1)
    start_row = jnp.zeros((8, 1024), jnp.int32)
    for d in range(4):
        start_row = jnp.maximum(start_row, jnp.where(place_row >= starts[0, d], starts[0, d], 0))
    position = (place_row - start_row).astype(F32)
    for i in range(8):
        columns = pl.ds(128 * i, 128)
        angle = s.frequency[...] * position[0:1, 128 * i : 128 * i + 128]
        s.cosine[:, columns] = jnp.cos(angle)
        s.sine[:, columns] = jnp.sin(angle)
    for qb in range(4):
        first = start_row[0:1, qb * 256 : qb * 256 + 256]
        query = lax.broadcasted_iota(jnp.int32, (256, 256), 1) + qb * 256
        for kb in range(qb + 1):
            key = lax.broadcasted_iota(jnp.int32, (256, 256), 0) + kb * 256
            allowed = (key <= query) & (key >= first)
            s.dgu[pl.ds(256 * kb, 256), pl.ds(256 * qb, 256)] = jnp.where(allowed, 1.0, 0.0).astype(BF16)

    s.gain1[...] = jnp.broadcast_to(s.g1_in[...], (128, 1024)).T
    s.gain2[...] = jnp.broadcast_to(s.g2_in[...], (128, 1024)).T
    s.gain_q[...] = jnp.broadcast_to(s.gq_in[...], (128, 128)).T
    s.gain_k[...] = jnp.broadcast_to(s.gk_in[...], (128, 128)).T
    s.gain_q_sum[...] = jnp.zeros((128, 128), F32)
    s.gain_sum[...] = jnp.zeros((1024, 128), F32)
    s.gain_k_sum[...] = jnp.zeros((128, 256), F32)
    for g in range(2):
        s.v_t[g, pl.ds(128, 16), :] = jnp.ones((16, 1024), BF16)

    def x_in(i, total):
        turned = s.x_in[:, span(i)].astype(F32).T
        s.x_t[span(i), :] = turned.astype(BF16)
        return total + fold(turned * turned)

    square = lax.fori_loop(0, 4, x_in, jnp.zeros((8, BLOCK), F32))
    root = lax.rsqrt(jnp.sum(square, axis=0, keepdims=True) / 1024.0 + EPSILON)
    s.root1[...] = jnp.broadcast_to(root, (8, BLOCK))

    loads[8].wait()

    def turn_out(i):
        s.attn_mix[i, :, :, pl.ds(1024, 512)] = s.h2[pl.ds(0, 512), span(i)].T.reshape(4, 64, 512)

    loop(4, turn_out)
    loads[9].wait()
    loads[10].wait()

    def turn_gu(i):
        for z in range(4):
            turned = s.mlp_mix[z, :, :, span(i)].reshape(256, 256).T
            s.t_gu[i, :, :, pl.ds(256 * z, 256)] = turned.reshape(4, 64, 256)

    loop(6, turn_gu)
    loads[11].wait()

    def turn_down(i):
        s.mlp_mix[i, :, :, pl.ds(1536, 768)] = s.w_down[:, span(i)].T.reshape(4, 64, 768)

    loop(4, turn_down)

    def dy_in(i):
        s.attn_mix[i, :, :, span(me)] = s.da[pl.ds(0, 256), span(i)].T.reshape(4, 64, BLOCK)

    loads[12].wait()
    loop(4, dy_in)

    def project(blocks, part):
        cosine, sine = pair(s.cosine, pl.ds(0, 64), blocks, part), pair(s.sine, pl.ds(0, 64), blocks, part)
        query_gain = twice(s.gain_q[...] * QUERY_SCALE)
        key_gain = twice(s.gain_k[...])
        every_raw = nn(s.t_qkv[...], pair(s.h1, every, blocks, part))
        for g in range(2):
            raw = every_raw[512 * g : 512 * g + 512]
            for k in range(2):
                head = 3 * g + k
                normed, root, turned = head_forward(raw[128 * k : 128 * k + 128], query_gain, cosine, sine)
                unpair(s.norm_qk, pl.ds(128 * head, 128), blocks, part, normed.astype(BF16))
                unpair(s.root_qk, pl.ds(head, 1), blocks, part, root)
                turned = turned.astype(BF16)
                for n, b in enumerate(blocks):
                    s.qs[g, b, :, lanes(2 * part + k)] = turned[:, HALF * n : HALF * n + HALF]
            normed, root, turned = head_forward(raw[256:384], key_gain, cosine, sine)
            turned, values = turned.astype(BF16), raw[384:].astype(BF16)
            unpair(s.norm_qk, pl.ds(384 * g + 256, 128), blocks, part, normed.astype(BF16))
            unpair(s.root_qk, pl.ds(3 * g + 2, 1), blocks, part, root)
            unpair(s.ks_t, pl.ds(128 * g, 128), blocks, part, turned)
            for n, b in enumerate(blocks):
                s.v_t[g, pl.ds(0, 128), sub(b, part)] = values[:, HALF * n : HALF * n + HALF]
                s.ks[g, sub(b, part), :] = turned[:, HALF * n : HALF * n + HALF].T
                s.v[g, sub(b, part), :] = values[:, HALF * n : HALF * n + HALF].T

    def both_roles(own, body):
        for far in range(2):
            blocks = (2 * far, 2 * far + 1) if own else (2 - 2 * far, 3 - 2 * far)
            pl.when(place.far == far)(lambda blocks=blocks: body(blocks))

    def p_slots(g, qb):
        return pl.ds(g * 10 + qb * (qb + 1) // 2, qb + 1)

    def attend(blocks, parts):
        wide = 256 * len(parts)
        cut = lanes(parts[0], 256) if len(parts) == 1 else pl.ds(0, wide)
        chains = [(qb, g, 256 * (qb + 1)) for qb in blocks for g in range(2)]
        scores = [nn(s.ks[g, pl.ds(0, keys), :], s.qs[g, qb, :, cut]) for qb, g, keys in chains]
        weights = []
        for (qb, g, keys), score in zip(chains, scores):
            halves = [twice(s.dgu[pl.ds(0, keys), lanes(2 * qb + part)]) for part in parts]
            mask = halves[0] if len(parts) == 1 else jnp.concatenate(halves, axis=1)
            weights.append(jnp.exp2(score).astype(BF16) * mask)
        products = [nn(s.v_t[g, :, pl.ds(0, keys)], weight) for (qb, g, keys), weight in zip(chains, weights)]
        for (qb, g, keys), weight, product in zip(chains, weights, products):
            s.p[p_slots(g, qb), :, :, cut] = weight.reshape(qb + 1, 4, 64, wide)
            inverse = 1.0 / product[128:136]
            s.inv[g, qb, :, cut] = inverse
            attended = (product[:128] * inverse[0:1]).astype(BF16)
            for n, part in enumerate(parts):
                for k in range(2):
                    columns = slice(256 * n + 128 * k, 256 * n + 128 * k + 128)
                    s.ob[pl.ds(256 * g + 128 * k, 128), lanes(2 * qb + part)] = attended[:, columns]

    def out_product(blocks, part, store):
        attended = pair(s.ob, pl.ds(0, 512), blocks, part)
        store(nn(s.attn_mix[:, :, :, pl.ds(1024, 512)].reshape(1024, 512), attended))

    def split(sib_out, index, part, keep):
        def store(values):
            sib_out[index, part] = values[:, :HALF].astype(BF16)
            keep[:, lanes(part)] = values[:, HALF:]

        return store

    gather_dy = Gather(links, lambda b, part: s.attn_mix.at[:, :, :, sub(b, part)])

    def choose(far):
        return tuple(jnp.where(far, b, a) for a, b in zip(near_pair, far_pair))

    def project_step(k, when):
        when(0, lambda: gather_h1.near_ready(0))
        when(1, lambda: gather_h1.near_ready(1))

        def third():
            gather_h1.pass_on(0)
            gather_h1.far_ready(0)

        when(2, third)

        def fourth():
            gather_h1.pass_on(1)
            for part in range(2):
                gather_dy.send_near(part)
            gather_dy.send_far(0)
            gather_h1.far_ready(1)

        when(3, fourth)
        project(choose(k >= 2), k % 2)

    steps(4, project_step)

    sum_attn = Reduce(links, s.sib_out, s.sib_in, s.far_out, s.far_in)

    def attend_step(k, when):
        both_roles(False, lambda blocks: attend(blocks, (k,)))

        def second():
            sum_attn.make_far(s.keep_far, 0)
            sum_attn.send_far(0)

        when(1, second)
        out_product(far_pair, k, split(s.sib_out, 0, k, s.keep_far))
        when(0, lambda: sum_attn.to_sibling(0, 0))
        when(1, lambda: sum_attn.to_sibling(0, 1))

    steps(2, attend_step)
    both_roles(True, lambda blocks: attend(blocks, (0, 1)))
    sum_attn.make_far(s.keep_far, 1)
    sum_attn.send_far(1)
    loop(2, lambda part: out_product(near_pair, part, split(s.sib_out, 1, part, s.keep_own)))
    for part in range(2):
        sum_attn.to_sibling(1, part)
    for part in range(2):
        gather_dy.near_ready(part)
    gather_dy.pass_on(0)

    gather_h2 = Gather(links, lambda b, part: s.h2.at[:, sub(b, part)])

    def second_norm(part):
        sum_attn.arrive(part)

        def square(i, total):
            x1 = s.x_t[span(i), lanes(part)].astype(F32) + sum_attn.total(s.keep_own, part, span(i))
            s.resid[span(i), lanes(part)] = x1
            return total + fold(x1 * x1)

        total = lax.fori_loop(0, 4, square, jnp.zeros((8, HALF), F32))
        root = lax.rsqrt(jnp.sum(total, axis=0, keepdims=True) / 1024.0 + EPSILON)
        s.root2[:, lanes(part)] = jnp.broadcast_to(root, (8, HALF))

        def scale(i):
            normed = s.resid[span(i), lanes(part)] * s.root2[0:1, lanes(part)]
            s.h2[span(i), sub(me, part)] = (normed * s.gain2[span(i), :]).astype(BF16)

        loop(4, scale)
        gather_h2.send(part)

    def feed(blocks, part):
        def body(j):
            gate = nn(s.t_gu[j].reshape(256, 1024), pair(s.h2, every, blocks, part))
            up = nn(s.t_gu[3 + j].reshape(256, 1024), pair(s.h2, every, blocks, part))
            grads = [s.attn_mix[:, :, :, sub(b, part)].reshape(1024, HALF) for b in blocks]
            grad = nn(s.w_down[span(j), :], jnp.concatenate(grads, axis=1))
            open_gate = jax.nn.sigmoid(gate)
            silu = gate * open_gate
            unpair(s.hidden, span(j), blocks, part, (silu * up).astype(BF16))
            dgate = (grad * up * open_gate * (1.0 + gate * (1.0 - open_gate))).astype(BF16)
            unpair(s.dgu, span(j), blocks, part, dgate)
            unpair(s.dgu, span(3 + j), blocks, part, (grad * silu).astype(BF16))

        for j in range(3):
            body(j)

    def feed_back(blocks, part, store):
        grads = pair(s.dgu, pl.ds(0, 1536), blocks, part)
        store(nn(s.mlp_mix[:, :, :, pl.ds(0, 1536)].reshape(1024, 1536), grads))

    def mlp_product(blocks, part, store):
        hidden = pair(s.hidden, pl.ds(0, 768), blocks, part)
        store(nn(s.mlp_mix[:, :, :, pl.ds(1536, 768)].reshape(1024, 768), hidden))

    sum_dh2 = Reduce(links, s.sib_out, s.sib_in, s.far_out, s.far_in)

    def feed_step(k, when):
        def first():
            second_norm(0)
            sum_attn.release(1, 0)
            gather_h2.near_ready(0)

        when(0, first)

        def second():
            second_norm(1)
            sum_attn.drain()
            gather_h2.pass_on(0)
            gather_h2.near_ready(1)

        when(1, second)

        def third():
            gather_dy.far_ready(0)
            gather_h2.far_ready(0)

        when(2, third)

        def fourth():
            gather_h2.pass_on(1)
            gather_dy.pass_on(1)
            gather_h2.far_ready(1)
            gather_dy.far_ready(1)

        when(3, fourth)
        far, part = k >= 2, k % 2
        feed(choose(far), part)
        index = 1 - k // 2
        feed_back(choose(far), part, split(s.sib_out, index, part, s.keep.at[index]))
        when(0, lambda: sum_dh2.to_sibling(1, 0))

        def second_end():
            sum_dh2.to_sibling(1, 1)
            gather_dy.send_far(1)

        when(1, second_end)

        def third_end():
            sum_dh2.to_sibling(0, 0)
            sum_dh2.make_far(s.keep_far, 0)
            sum_dh2.send_far(0)

        when(2, third_end)
        when(3, lambda: sum_dh2.to_sibling(0, 1))

    steps(4, feed_step)

    dp_mlp = DpSum(links, s, MLP_STREAMS, s.mlp_halves)

    def feed_grad(stream):
        name, first, w, _, _, _, _ = MLP_STREAMS[stream]
        if name == "mlp_mix":
            values = nt(s.h2[...], s.dgu[pl.ds(first, w), :])
        else:
            values = nt(s.attn_mix[:, :, :, pl.ds(0, 1024)].reshape(1024, 1024), s.hidden[pl.ds(first, w), :])
        into = getattr(s, name)
        into[pl.ds(0, 4), :, :, pl.ds(first, w)] = values.astype(BF16).reshape(4, 4, 64, w)
        dp_mlp.start(stream)

    gather_da = Gather(links, lambda b, part: s.da.at[:, sub(b, part)])

    def norm_back(part):
        sum_dh2.arrive(part)

        def inner_sum(i, total):
            grad = sum_dh2.total(s.keep_own, part, span(i))
            s.keep_own[span(i), lanes(part)] = grad
            product = grad * (s.resid[span(i), lanes(part)] * s.root2[0:1, lanes(part)])
            s.gain_sum[span(i), :] += product
            return total + fold(product * s.gain2[span(i), :])

        inner = lax.fori_loop(0, 4, inner_sum, jnp.zeros((8, HALF), F32))
        inner = jnp.sum(inner, axis=0, keepdims=True) / 1024.0

        def body(i):
            root = s.root2[0:1, lanes(part)]
            scaled = s.keep_own[span(i), lanes(part)] * s.gain2[span(i), :]
            normed = s.resid[span(i), lanes(part)] * root
            own = s.attn_mix[i, :, :, sub(me, part)].reshape(256, HALF).astype(F32)
            s.da[span(i), sub(me, part)] = (own + root * (scaled - normed * inner)).astype(BF16)
            s.mlp_own[span(i), lanes(part)] = s.resid[span(i), lanes(part)]
            s.resid[span(i), lanes(part)] = own + root * (scaled - normed * inner)

        loop(4, body)
        gather_da.send(part)

    feed_grad(0)
    sum_dh2.make_far(s.keep_far, 1)
    sum_dh2.send_far(1)
    feed_grad(1)
    norm_back(0)
    feed_grad(4)
    feed_grad(2)
    feed_grad(3)
    gather_h2.drain()
    load(wo, s.h2.at[pl.ds(0, 512)])
    norm_back(1)
    sum_dh2.drain()

    def put_gain(first, row):
        for k in range(row.shape[1] // 128):
            s.gain_own[first + k : first + k + 1, :] = row[:, 128 * k : 128 * k + 128]

    put_gain(8, jnp.sum(s.gain_sum[...].T, axis=0, keepdims=True))
    s.gain_sum[...] = jnp.zeros((1024, 128), F32)

    sum_mlp = Reduce(links, s.mlp_sib_out, s.mlp_sib_in, s.mlp_far_out, s.mlp_far_in)

    def mlp_mine(part):
        def store(values):
            s.mlp_sib_out[1, part] = values[:, :HALF].astype(BF16)
            s.mlp_own[:, lanes(part)] += values[:, HALF:]

        return store

    loop(2, lambda part: mlp_product(far_pair, part, split(s.mlp_sib_out, 0, part, s.keep_far)))
    for part in range(2):
        sum_mlp.to_sibling(0, part)
    for part in range(2):
        sum_mlp.make_far(s.keep_far, part)

    s.keep[...] = jnp.zeros((2, 1024, 256), F32)
    loads[17].wait()

    def dob(g, b, part):
        index = g * 4 + b
        return (4 + index // 4, pl.ds(2 * ((index // 2) % 2), 2), slice(None), pl.ds(pl.multiple_of((index % 2) * 512 + part * 256, 256), 256))

    def out_back(blocks, part):
        two = lanes(part, 256)
        every_grad = nn(s.h2[pl.ds(0, 512), :], pair(s.da, every, blocks, part))
        for g in range(2):
            grads = every_grad[256 * g : 256 * g + 256]
            for n, b in enumerate(blocks):
                columns = slice(HALF * n, HALF * n + HALF)
                both = jnp.concatenate([grads[:128, columns], grads[128:, columns]], axis=1) * s.inv[g, b, 0:1, two]
                outs = [s.ob[pl.ds(256 * g + 128 * k, 128), sub(b, part)] for k in range(2)]
                inner = jnp.sum(both * jnp.concatenate(outs, axis=1).astype(F32), axis=0, keepdims=True)
                s.inner[g, b, :, two] = jnp.broadcast_to(inner, (8, 256))
                s.t_gu[dob(g, b, part)] = both.astype(BF16).reshape(2, 64, 256)

    def attend_back(blocks, parts, groups):
        wide = 256 * len(parts)
        cut = lanes(parts[0], 256) if len(parts) == 1 else pl.ds(0, wide)
        chains = [(qb, g, 256 * (qb + 1)) for qb in blocks for g in groups]
        grads, weights, slopes, changes, key_parts, query_parts, value_parts = [], [], [], [], [], [], []
        for qb, g, keys in chains:
            index = g * 4 + qb
            columns = lanes((index % 2) * 2 + parts[0], 256) if len(parts) == 1 else lanes(index % 2, 512)
            at = (4 + index // 4, pl.ds(2 * ((index // 2) % 2), 2), slice(None), columns)
            grads.append(s.t_gu[at].reshape(128, wide))
            weights.append(s.p[p_slots(g, qb), :, :, cut].reshape(keys, wide))
        for (qb, g, keys), grad in zip(chains, grads):
            slopes.append(nn(s.v[g, pl.ds(0, keys), :], grad))
        for weight, grad in zip(weights, grads):
            value_parts.append(nt(weight, grad))
        for (qb, g, keys), weight, slope in zip(chains, weights, slopes):
            changes.append((weight.astype(F32) * (slope - s.inner[g, qb, 0:1, cut])).astype(BF16))
        for (qb, g, keys), change in zip(chains, changes):
            key_parts.append(nt(change, s.qs[g, qb, :, cut]))
            query_parts.append(nn(s.ks_t[pl.ds(128 * g, 128), pl.ds(0, keys)], change))
        for (qb, g, keys), value_part, key_part, query_part in zip(chains, value_parts, key_parts, query_parts):
            s.keep_own[pl.ds(0, keys), lanes(g)] += value_part
            s.keep_far[pl.ds(0, keys), lanes(g)] += key_part
            for n, part in enumerate(parts):
                columns = lanes(2 * qb + part)
                for k in range(2):
                    head = 3 * g + k
                    grad, gain_part = head_backward(
                        query_part[:, 256 * n + 128 * k : 256 * n + 128 * k + 128] * (1.0 / math.sqrt(HEAD)),
                        s.norm_qk[pl.ds(128 * head, 128), columns].astype(F32),
                        s.root_qk[pl.ds(head, 1), columns],
                        s.gain_q[...],
                        s.cosine[:, columns],
                        s.sine[:, columns],
                    )
                    s.t_qkv[pl.ds(512 * g + 128 * k, 128), columns] = grad.astype(BF16)
                    s.gain_q_sum[...] += gain_part

    def key_back(g):
        gain = twice(s.gain_k[...])

        def body(b):
            columns = span(b)
            grad, gain_part = head_backward(
                s.keep_far[columns, lanes(g)].T * math.log(2.0),
                s.norm_qk[pl.ds(384 * g + 256, 128), columns].astype(F32),
                s.root_qk[pl.ds(3 * g + 2, 1), columns],
                gain,
                s.cosine[:, columns],
                s.sine[:, columns],
            )
            s.t_qkv[pl.ds(512 * g + 256, 128), columns] = grad.astype(BF16)
            s.gain_k_sum[...] += gain_part
            s.t_qkv[pl.ds(512 * g + 384, 128), columns] = s.keep_own[columns, lanes(g)].T.astype(BF16)

        loop(4, body)

    def tell_ready():
        for k, name in enumerate(PARTNERS[2:]):
            pl.semaphore_signal(ready.at[k], inc=1, device_id=place.device(name), device_id_type=MESH)

    def wait_ready():
        for k in range(5):
            pl.semaphore_wait(ready.at[k], 1)

    def qkv_grad(g):
        values = nt(s.h1[...], s.t_qkv[span(g, 512), :]).astype(BF16)
        s.attn_mix[:, :, :, span(g, 512)] = values.reshape(4, 4, 64, 512)

    def out_grad():
        values = nt(s.da[...], s.ob[...]).astype(BF16)
        s.attn_mix[:, :, :, pl.ds(1024, 512)] = values.reshape(4, 4, 64, 512)

    for part in range(2):
        gather_da.near_ready(part)
    loop(2, lambda part: out_back(near_pair, part))
    gather_da.pass_on(0)
    both_roles(True, lambda blocks: attend_back(blocks, (0, 1), (0, 1)))
    gather_dy.drain()

    def back_step(k, when):
        when(0, lambda: gather_da.far_ready(0))
        when(1, lambda: gather_da.far_ready(1))
        out_back(far_pair, k)

        def first():
            gather_da.pass_on(1)
            sum_mlp.send_far(0)

        when(0, first)
        when(1, dp_mlp.advance)
        both_roles(False, lambda blocks: attend_back(blocks, (k,), (0, 1)))

    steps(2, back_step)
    tell_ready()
    for g in range(2):
        key_back(g)
    out_grad()
    loop(2, qkv_grad)
    wait_ready()
    dp_attn = DpSum(links, s, ATTN_STREAMS, s.p)
    dp_attn.start(0, 1, 2, 3)

    def in_back(blocks, part, store):
        values = nn(s.w_qkv[...], pair(s.t_qkv, every, blocks, part))
        product = values * pair(s.h1, every, blocks, part).astype(F32)
        s.gain_sum[...] += product[:, :HALF] + product[:, HALF:]
        store(values)

    sum_dh1 = Reduce(links, s.sib_out, s.sib_in, s.far_out, s.far_in)
    loop(2, lambda part: in_back(far_pair, part, split(s.sib_out, 0, part, s.keep_far)))
    for part in range(2):
        sum_dh1.to_sibling(0, part)
    for part in range(2):
        sum_dh1.make_far(s.keep_far, part)
        sum_dh1.send_far(part)
    sum_mlp.send_far(1)
    dp_mlp.advance()
    loop(2, lambda part: in_back(near_pair, part, split(s.sib_out, 1, part, s.keep_own)))
    for part in range(2):
        sum_dh1.to_sibling(1, part)
    loop(2, lambda part: mlp_product(near_pair, part, mlp_mine(part)))
    for part in range(2):
        sum_mlp.to_sibling(1, part)
    put_gain(0, jnp.sum((s.gain_sum[...] / s.gain1[...]).T, axis=0, keepdims=True))
    both = s.gain_k_sum[:, lanes(0)] + s.gain_k_sum[:, lanes(1)]
    put_gain(16, jnp.sum(s.gain_q_sum[...].T, axis=0, keepdims=True))
    put_gain(17, jnp.sum(both.T, axis=0, keepdims=True))
    s.gain_own[pl.ds(18, 6), :] = jnp.zeros((6, 128), F32)
    gains = GainSum(links, s.gain_own, s.gain_parts)
    dp_attn.advance()
    dp_mlp.advance()
    gains.advance()
    dp_attn.advance()
    dp_mlp.advance()
    gains.advance()

    for part in range(2):
        sum_dh1.arrive(part)

        def inner_sum(i, total, part=part):
            grad = sum_dh1.total(s.keep_own, part, span(i))
            s.keep_own[span(i), lanes(part)] = grad
            normed = s.x_t[span(i), lanes(part)].astype(F32) * s.root1[0:1, lanes(part)]
            return total + fold(grad * normed * s.gain1[span(i), :])

        inner = lax.fori_loop(0, 4, inner_sum, jnp.zeros((8, HALF), F32))
        inner = jnp.sum(inner, axis=0, keepdims=True) / 1024.0

        def last_back(i, part=part, inner=inner):
            root = s.root1[0:1, lanes(part)]
            scaled = s.keep_own[span(i), lanes(part)] * s.gain1[span(i), :]
            normed = s.x_t[span(i), lanes(part)].astype(F32) * root
            s.resid[span(i), lanes(part)] += root * (scaled - normed * inner)

        loop(4, last_back)
        if part == 0:
            dp_attn.advance()
            gains.advance()
    load(s.resid, grad_x)

    for part in range(2):
        sum_mlp.arrive(part)

        def layer_out(i, part=part):
            s.stage[lanes(part), span(i)] = sum_mlp.total(s.mlp_own, part, span(i)).T.astype(BF16)

        loop(4, layer_out)
    load(s.stage, out)
    while dp_attn.phase < 5 or dp_mlp.phase < 5 or gains.step < 4:
        dp_attn.advance()
        gains.advance()
        dp_mlp.advance()
    load(s.sums, out_sums)
    s.gain_own[...] = gains.total
    load(s.gain_own, out_gains)

    for copy in loads[18:]:
        copy.wait()
    for exchange in (gather_h1, gather_da, sum_mlp, sum_dh1, dp_mlp, dp_attn, gains):
        exchange.drain()


def deliver_kernel(*refs):
    given, outs, held = refs[:4], refs[4:17], refs[17:21]
    turned, gain_rows, sems_in, sems_out = refs[21:]
    arrivals = [pltpu.make_async_copy(a, b, sems_in.at[k]) for k, (a, b) in enumerate(zip(given, held))]
    for copy in arrivals:
        copy.start()
    started = []

    def send(src, dst):
        copy = pltpu.make_async_copy(src, dst, sems_out.at[len(started)])
        copy.start()
        started.append(copy)

    arrivals[3].wait()
    gain_rows[0] = held[3][16:17]
    gain_rows[1] = held[3][17:18]
    send(held[3].at[pl.ds(0, 8)], outs[9])
    send(held[3].at[pl.ds(8, 8)], outs[10])
    send(gain_rows.at[0], outs[11])
    send(gain_rows.at[1], outs[12])
    arrivals[2].wait()
    sums = held[2]
    for g in range(2):
        for out, first, width in ((outs[2], 0, 256), (outs[3], 256, 128), (outs[4], 384, 128)):
            send(sums.at[:, pl.ds(512 * g + first, width)], out.at[:, pl.ds(width * g, width)])
    for out, first, width in ((outs[5], 1024, 512), (outs[6], 1536, 768), (outs[7], 2304, 768), (outs[8], 3072, 768)):
        send(sums.at[:, pl.ds(first, width)], out)
    arrivals[0].wait()
    send(held[0], outs[0])
    arrivals[1].wait()
    for i in range(4):
        turned[:, pl.ds(256 * i, 256)] = held[1][pl.ds(256 * i, 256), :].T
    send(turned, outs[1])
    for copy in started:
        copy.wait()


def shards(
    tokens,
    doc_starts,
    cotangent,
    w_query,
    key_matrix,
    value_matrix,
    w_out,
    w_gate,
    w_up,
    w_down,
    gain_attn,
    gain_mlp,
    gain_query,
    gain_key,
):
    frequency = ROPE_BASE ** (-(np.arange(64, dtype=np.float64) * 2.0) / HEAD)
    frequency = jnp.asarray(np.broadcast_to(frequency[:, None], (64, 128)).astype(np.float32))
    hbm = pl.BlockSpec(memory_space=pl.ANY)
    smem = pl.BlockSpec(memory_space=pltpu.SMEM)

    def shaped(*shape, kind=F32):
        return jax.ShapeDtypeStruct(shape, kind)

    gains = (shaped(8, 128), shaped(8, 128), shaped(1, 128), shaped(1, 128))
    given = (shaped(256, 1024, kind=BF16), shaped(1024, 256), shaped(32, 3840), shaped(24, 128))
    widths = (512, 256, 256, 512, 768, 768, 768)
    outs = pl.pallas_call(
        layer_kernel,
        out_shape=given,
        in_specs=[hbm, smem] + [hbm] * 13,
        out_specs=(hbm,) * 4,
        scratch_shapes=[pltpu.VMEM(shape, kind) for _, shape, kind in SCRATCH]
        + [
            pltpu.SemaphoreType.DMA((2, SEMAPHORES)),
            pltpu.SemaphoreType.DMA((24,)),
            pltpu.SemaphoreType.REGULAR((5,)),
        ],
        compiler_params=pltpu.CompilerParams(
            collective_id=0, has_side_effects=True, vmem_limit_bytes=64 * 2**20 - 2**16
        ),
        cost_estimate=pl.CostEstimate(flops=32 * 10**9, bytes_accessed=2**24, transcendentals=2**22),
        name="layer",
    )(
        tokens.reshape(256, 1024),
        doc_starts,
        cotangent.reshape(256, 1024),
        w_query,
        key_matrix,
        value_matrix,
        w_out,
        w_gate.reshape(4, 4, 64, 768),
        w_up.reshape(4, 4, 64, 768),
        w_down,
        gain_attn.reshape(1, 1024),
        gain_mlp.reshape(1, 1024),
        gain_query.reshape(1, 128),
        gain_key.reshape(1, 128),
        frequency,
    )
    outs = pl.pallas_call(
        deliver_kernel,
        out_shape=(given[0], shaped(256, 1024)) + tuple(shaped(32, width) for width in widths) + gains,
        in_specs=[hbm] * 4,
        out_specs=(hbm,) * 13,
        scratch_shapes=[pltpu.VMEM(one.shape, one.dtype) for one in given]
        + [
            pltpu.VMEM((256, 1024), F32),
            pltpu.VMEM((2, 1, 128), F32),
            pltpu.SemaphoreType.DMA((4,)),
            pltpu.SemaphoreType.DMA((16,)),
        ],
        name="deliver",
    )(*outs)
    return (
        outs[0].reshape(1, 256, 1024),
        outs[1].reshape(1, 256, 1024),
        *outs[2:5],
        outs[5].T,
        *outs[6:8],
        outs[8].T,
        *(gain.reshape(-1) for gain in outs[9:]),
    )


def solution(mesh):
    in_specs = (
        P("dp", "tensor", None),
        P("dp", None),
        P("dp", "tensor", None),
        P(None, "tensor"),
        P(None, "tensor"),
        P(None, "tensor"),
        P("tensor", None),
        P(None, "tensor"),
        P(None, "tensor"),
        P("tensor", None),
        P(),
        P(),
        P(),
        P(),
    )
    out_specs = (
        P("dp", "tensor", None),
        P("dp", "tensor", None),
        P("dp", "tensor"),
        P("dp", "tensor"),
        P("dp", "tensor"),
        P("tensor", "dp"),
        P("dp", "tensor"),
        P("dp", "tensor"),
        P("tensor", "dp"),
        P(),
        P(),
        P(),
        P(),
    )
    return jax.shard_map(shards, mesh=mesh, in_specs=in_specs, out_specs=out_specs, check_vma=False)
```

profile of v0, /device:TPU:6, one launch (start us, length us, event | category | flops | bytes accessed | tf_op | source)
XLA Modules:
  0.0 131.5 jit_solution(14853892324876629764)
XLA Ops:
  0.7 127.6 %layer.1 = (bf16[256,1024]{1,0:T(8,128)(2,1)}, f32[1024,256]{1,0:T(8,128)}, f32[32,3840]{1,0:T(8,128)}, f32[24,128]{1,0:T(8,128)}) custom-call(bf16[256,1024]{1,0:T(8,128)(2,1)} %bitcast.19, s32[1,4]{1,0:T(1,128)} %starts.1, bf16[256,1024]{1,0:T(8,128)(2,1)} %bitcast.20, bf16[1024,512]{1,0:T(8,128)(2,1)} %wq.1, bf16[1024,256]{1,0:T(8,128)(2,1)} %wk.1, ...), custom_call_target="tpu_custom_call" | custom-call | flops 32000000000 | bytes 16777216 | tf_op jit(solution)/shard_map/layer/pallas_call | solution.py:1169
  128.3 3.0 %deliver.1 = (bf16[256,1024]{1,0:T(8,128)(2,1)}, f32[256,1024]{1,0:T(8,128)}, f32[32,512]{1,0:T(8,128)}, f32[32,256]{1,0:T(8,128)}, f32[32,256]{1,0:T(8,128)}, /...) custom-call(bf16[256,1024]{1,0:T(8,128)(2,1)} %get-tuple-element.30., ...), custom_call_target="tpu_custom_call" | custom-call | tf_op jit(solution)/shard_map/deliver/pallas_call | solution.py:1202
where the time goes:
time: 132 us; the launch traced here: 131 us
  Pallas kernels  131 us (99%)
    pallas_call x1, Pallas kernels, shards(): pl.pallas_call(layer_kernel, out_shape=given, in_specs=[hbm, smem] + [hbm...  128 us
    pallas_call x1, Pallas kernels, shards(): pl.pallas_call(deliver_kernel, out_shape=(given[0], shaped(256, 1024)) +...  3 us

commit v1 on v0

--- a/solution.py
+++ b/solution.py
@@ -27,7 +27,9 @@
     ("t_gu", 0, 256, 8, 256, 2, 3072),
     ("t_gu", 256, 512, 12, 0, 3, 3328),
 )
-ATTN_STREAMS = tuple(("attn_mix", 384 * k, 384, 4 * k, 0, k, 384 * k) for k in range(4))
+ATTN_STREAMS = tuple(
+    ("attn_mix", 512 + 256 * k, 256, 10 + 4 * (k // 2), 256 * (k % 2), k, 512 + 256 * k) for k in range(4)
+) + tuple(("attn_mix", 128 * k, 128, 0, 128 * k, k, 128 * k) for k in range(4))
 GAIN_ORDER = ("y", "z", "tensor", "x")
 
 SCRATCH = (
@@ -88,7 +90,7 @@
     ("gain_own", (24, 128), F32),
     ("gain_parts", (4, 4, 24, 128), F32),
 )
-SEMAPHORES = 160
+SEMAPHORES = 190
 
 
 class Box:
@@ -311,7 +313,7 @@
     def __init__(self, links, box, streams, bufs):
         self.links, self.bufs, self.out = links, bufs, box.sums
         self.streams = [(getattr(box, name), *rest) for name, *rest in streams]
-        self.phase = -1
+        self.phases = [-1] * len(streams)
         self.flying = [[] for _ in streams]
         self.sent = []
 
@@ -393,21 +395,18 @@
     def start(self, *streams):
         for stream in streams:
             self.flying[stream] = self.begin(stream, 0)
-        self.phase = 0
-
-    def advance(self):
-        if self.phase == 5:
-            return
-        for stream in range(len(self.streams)):
-            self.finish(stream, self.phase)
+            self.phases[stream] = 0
+
+    def advance(self, *streams):
+        for stream in streams or range(len(self.streams)):
+            phase = self.phases[stream]
+            if phase == 5:
+                continue
+            self.finish(stream, phase)
             self.sent += self.flying[stream]
-            if self.phase < 4:
-                self.flying[stream] = self.begin(stream, self.phase + 1)
-        self.phase += 1
-
-    def complete(self):
-        while self.phase < 5:
-            self.advance()
+            if phase < 4:
+                self.flying[stream] = self.begin(stream, phase + 1)
+            self.phases[stream] = phase + 1
 
     def drain(self):
         for copy in self.sent:
@@ -1014,13 +1013,15 @@
 
     steps(2, back_step)
     tell_ready()
-    for g in range(2):
-        key_back(g)
     out_grad()
-    loop(2, qkv_grad)
+    key_back(1)
+    qkv_grad(1)
     wait_ready()
     dp_attn = DpSum(links, s, ATTN_STREAMS, s.p)
     dp_attn.start(0, 1, 2, 3)
+    key_back(0)
+    qkv_grad(0)
+    dp_attn.start(4, 5, 6, 7)
 
     def in_back(blocks, part, store):
         values = nn(s.w_qkv[...], pair(s.t_qkv, every, blocks, part))
@@ -1088,7 +1089,7 @@
 
         loop(4, layer_out)
     load(s.stage, out)
-    while dp_attn.phase < 5 or dp_mlp.phase < 5 or gains.step < 4:
+    while min(dp_attn.phases + dp_mlp.phases) < 5 or gains.step < 4:
         dp_attn.advance()
         gains.advance()
         dp_mlp.advance()
@@ -1105,8 +1106,13 @@
 def deliver_kernel(*refs):
     given, outs, held = refs[:4], refs[4:17], refs[17:21]
     turned, gain_rows, sems_in, sems_out = refs[21:]
-    arrivals = [pltpu.make_async_copy(a, b, sems_in.at[k]) for k, (a, b) in enumerate(zip(given, held))]
-    for copy in arrivals:
+    arrivals = {k: pltpu.make_async_copy(given[k], held[k], sems_in.at[k]) for k in (0, 2, 3)}
+    pieces = []
+    for i in range(4):
+        rows = pl.ds(256 * i, 256)
+        pieces.append(pltpu.make_async_copy(given[1].at[rows], held[1].at[rows], sems_in.at[4 + i]))
+        pieces[i].start()
+    for copy in arrivals.values():
         copy.start()
     started = []
 
@@ -1115,6 +1121,11 @@
         copy.start()
         started.append(copy)
 
+    for i in range(4):
+        columns = pl.ds(256 * i, 256)
+        pieces[i].wait()
+        turned[:, columns] = held[1][columns, :].T
+        send(turned.at[:, columns], outs[1].at[:, columns])
     arrivals[3].wait()
     gain_rows[0] = held[3][16:17]
     gain_rows[1] = held[3][17:18]
@@ -1131,10 +1142,6 @@
         send(sums.at[:, pl.ds(first, width)], out)
     arrivals[0].wait()
     send(held[0], outs[0])
-    arrivals[1].wait()
-    for i in range(4):
-        turned[:, pl.ds(256 * i, 256)] = held[1][pl.ds(256 * i, 256), :].T
-    send(turned, outs[1])
     for copy in started:
         copy.wait()
 
@@ -1208,8 +1215,8 @@
         + [
             pltpu.VMEM((256, 1024), F32),
             pltpu.VMEM((2, 1, 128), F32),
-            pltpu.SemaphoreType.DMA((4,)),
-            pltpu.SemaphoreType.DMA((16,)),
+            pltpu.SemaphoreType.DMA((8,)),
+            pltpu.SemaphoreType.DMA((20,)),
         ],
         name="deliver",
     )(*outs)

time: 132 us -> 131 us (level)
  Pallas kernels: 131 us -> 129 us
where the time goes in v1:
time: 131 us; the launch traced here: 130 us
  Pallas kernels  129 us (98%)
    pallas_call x1, Pallas kernels, shards(): pl.pallas_call(layer_kernel, out_shape=given, in_specs=[hbm, smem] + [hbm...  127 us
    pallas_call x1, Pallas kernels, shards(): pl.pallas_call(deliver_kernel, out_shape=(given[0], shaped(256, 1024)) +...  2.8 us

profile of v1, /device:TPU:6, one launch (start us, length us, event | category | flops | bytes accessed | tf_op | source)
XLA Modules:
  0.0 130.2 jit_solution(8365824944894489017)
XLA Ops:
  0.7 126.6 %layer.1 = (bf16[256,1024]{1,0:T(8,128)(2,1)}, f32[1024,256]{1,0:T(8,128)}, f32[32,3840]{1,0:T(8,128)}, f32[24,128]{1,0:T(8,128)}) custom-call(bf16[256,1024]{1,0:T(8,128)(2,1)} %bitcast.19, s32[1,4]{1,0:T(1,128)} %starts.1, bf16[256,1024]{1,0:T(8,128)(2,1)} %bitcast.20, bf16[1024,512]{1,0:T(8,128)(2,1)} %wq.1, bf16[1024,256]{1,0:T(8,128)(2,1)} %wk.1, ...), custom_call_target="tpu_custom_call" | custom-call | flops 32000000000 | bytes 16777216 | tf_op jit(solution)/shard_map/layer/pallas_call | solution.py:1176
  127.3 2.8 %deliver.1 = (bf16[256,1024]{1,0:T(8,128)(2,1)}, f32[256,1024]{1,0:T(8,128)}, f32[32,512]{1,0:T(8,128)}, f32[32,256]{1,0:T(8,128)}, f32[32,256]{1,0:T(8,128)}, /...) custom-call(bf16[256,1024]{1,0:T(8,128)(2,1)} %get-tuple-element.30., ...), custom_call_target="tpu_custom_call" | custom-call | tf_op jit(solution)/shard_map/deliver/pallas_call | solution.py:1209

commit v2 on v1

--- a/solution.py
+++ b/solution.py
@@ -1044,6 +1044,7 @@
     loop(2, lambda part: mlp_product(near_pair, part, mlp_mine(part)))
     for part in range(2):
         sum_mlp.to_sibling(1, part)
+    dp_attn.advance(0, 1, 2, 3)
     put_gain(0, jnp.sum((s.gain_sum[...] / s.gain1[...]).T, axis=0, keepdims=True))
     both = s.gain_k_sum[:, lanes(0)] + s.gain_k_sum[:, lanes(1)]
     put_gain(16, jnp.sum(s.gain_q_sum[...].T, axis=0, keepdims=True))

time: 131 us -> 134 us (1.023)
  Pallas kernels: 129 us -> 132 us
    pallas_call x1, Pallas kernels: 127 us -> 129 us  [shards(): pl.pallas_call(layer_kernel, out_shape=given, in_specs=[hbm, smem] + [hbm...]
where the time goes in v2:
time: 134 us; the launch traced here: 133 us
  Pallas kernels  132 us (99%)
    pallas_call x1, Pallas kernels, shards(): pl.pallas_call(layer_kernel, out_shape=given, in_specs=[hbm, smem] + [hbm...  129 us
    pallas_call x1, Pallas kernels, shards(): pl.pallas_call(deliver_kernel, out_shape=(given[0], shaped(256, 1024)) +...  2.8 us

profile of v2, /device:TPU:6, one launch (start us, length us, event | category | flops | bytes accessed | tf_op | source)
XLA Modules:
  0.0 133.0 jit_solution(13770896914077484259)
XLA Ops:
  0.7 129.4 %layer.1 = (bf16[256,1024]{1,0:T(8,128)(2,1)}, f32[1024,256]{1,0:T(8,128)}, f32[32,3840]{1,0:T(8,128)}, f32[24,128]{1,0:T(8,128)}) custom-call(bf16[256,1024]{1,0:T(8,128)(2,1)} %bitcast.19, s32[1,4]{1,0:T(1,128)} %starts.1, bf16[256,1024]{1,0:T(8,128)(2,1)} %bitcast.20, bf16[1024,512]{1,0:T(8,128)(2,1)} %wq.1, bf16[1024,256]{1,0:T(8,128)(2,1)} %wk.1, ...), custom_call_target="tpu_custom_call" | custom-call | flops 32000000000 | bytes 16777216 | tf_op jit(solution)/shard_map/layer/pallas_call | solution.py:1177
  130.0 2.8 %deliver.1 = (bf16[256,1024]{1,0:T(8,128)(2,1)}, f32[256,1024]{1,0:T(8,128)}, f32[32,512]{1,0:T(8,128)}, f32[32,256]{1,0:T(8,128)}, f32[32,256]{1,0:T(8,128)}, /...) custom-call(bf16[256,1024]{1,0:T(8,128)(2,1)} %get-tuple-element.30., ...), custom_call_target="tpu_custom_call" | custom-call | tf_op jit(solution)/shard_map/deliver/pallas_call | solution.py:1210
